TPU v7x, 256 devices: a whole 4x4x8 slice. The times are simulated.
256 devices in a mesh: dp: 32 (over z, x), fsdp: 8 (over y, core).
Axes of the slice: x: 4, y: 4, z: 8, core: 2. Of those that a mesh axis runs over, the one named last changes fastest.
Arguments:
- incoming_feature_maps: bfloat16 [256, 8, 8, 3072], P('dp', None, None, 'fsdp'), may hold values from -6 to 6
- spatial_filter_tensor: bfloat16 [7, 7, 3072], P(None, None, 'fsdp'), may hold values from -0.875 to 0.875
- spatial_filter_offset: float32 [3072], P('fsdp'), may hold values from -3 to 3
- unit_layernorm_multiplier: float32 [3072], replicated, may hold values from 0.5 to 1.5
- unit_layernorm_offset_vector: float32 [3072], replicated, may hold values from -3 to 3
- expansion_linear_map: bfloat16 [3072, 12288], P('dp', 'fsdp'), may hold values from -0.109375 to 0.109375
- expansion_offset: float32 [12288], P('fsdp'), may hold values from -3 to 3
- contraction_linear_map: bfloat16 [12288, 3072], P('fsdp', 'dp'), may hold values from -0.109375 to 0.109375
- contraction_offset: float32 [3072], P('fsdp'), may hold values from -3 to 3
- residual_channel_factor: float32 [3072], P('fsdp'), may hold values from 0.3 to 1.5
- readout_layernorm_multiplier: float32 [3072], P('fsdp'), may hold values from 0.5 to 1.5
- readout_layernorm_offset: float32 [3072], P('fsdp'), may hold values from -3 to 3
- readout_linear_map: bfloat16 [3072, 768], P('fsdp'), may hold values from -0.109375 to 0.109375
- learner_caption_vectors: bfloat16 [16384, 768], P(('dp', 'fsdp')), may hold values from -6 to 6
- mentor_caption_vectors: bfloat16 [16384, 768], P(('dp', 'fsdp')), may hold values from -6 to 6
- mentor_picture_vectors: bfloat16 [256, 768], P('dp'), may hold values from -6 to 6
- divisor_per_slot: float32 [64], replicated, may hold values from 0.003 to 0.07
- active_program_slot: int32 [1], replicated, may hold values from 0 to 63
- matching_caption_slot: int32 [256], replicated, may hold values from 0 to 16383
Outputs:
- block_out: bfloat16 [256, 8, 8, 3072], P('dp', None, None, 'fsdp')
- embedding: float32 [256, 768], P('dp')
- losses: float32 [256], P(('dp', 'fsdp'))
All inputs are finite; a program needn't handle non-finite values.
Results may differ from a plain program's by a relative error of at most 0.015.
Values may be sent and summed in bfloat16 or wider, within the bound.
No kernel may reach another device: no remote copies, remote signals or barrier semaphores. Data moves between devices by JAX's collectives and lax.ppermute only.
A program may use at most 128 MiB of HBM per device.

v0:
```python
import jax
import jax.numpy as jnp
from jax import lax
from jax.experimental import pallas as pl
from jax.experimental.pallas import tpu as pltpu
from jax.sharding import PartitionSpec as P

SIDE = 8
KERNEL = 7
Z_SIDE = 8
X_SIDE = 4
Y_SIDE = 4
CORES = 2
X_GROUPS = [[z * X_SIDE + x for x in range(X_SIDE)] for z in range(Z_SIDE)]
Z_GROUPS = [[z * X_SIDE + x for z in range(Z_SIDE)] for x in range(X_SIDE)]


EPSILON = 1e-06
HIGHEST = lax.Precision.HIGHEST


def depthwise(incoming_feature_maps, spatial_filter_tensor, spatial_filter_offset):
    radius = KERNEL // 2
    padded = jnp.pad(
        incoming_feature_maps.astype(jnp.float32),
        ((0, 0), (radius, radius), (radius, radius), (0, 0)),
    )
    summed = jnp.zeros(incoming_feature_maps.shape, jnp.float32)
    for vertical in range(KERNEL):
        for horizontal in range(KERNEL):
            window = padded[:, vertical : vertical + SIDE, horizontal : horizontal + SIDE, :]
            summed = (
                summed + spatial_filter_tensor[vertical, horizontal].astype(jnp.float32) * window
            )
    return (summed + spatial_filter_offset).astype(jnp.bfloat16)


def unit_rows(values):
    return (values / jnp.sqrt(jnp.sum(values * values, -1, keepdims=True) + EPSILON)).astype(
        jnp.bfloat16
    )


def logits(queries, keys, divisor):
    return (
        lax.dot_general(
            queries, keys, (((1,), (1,)), ((), ())), preferred_element_type=jnp.float32
        )
        / divisor
    )


def broadcast_gather(value, axis):
    copies = jnp.broadcast_to(value[None], (lax.axis_size(axis),) + value.shape)
    return lax.all_to_all(copies, axis, 0, 0)


def split_product(values, weights):
    top = lax.reduce_precision(values, 8, 7)
    rest = values - top
    middle = lax.reduce_precision(rest, 8, 7)
    pieces = jnp.concatenate([top, middle, rest - middle], 0).astype(jnp.bfloat16)
    product = jnp.dot(pieces, weights, preferred_element_type=jnp.float32)
    rows = values.shape[0]
    return product[2 * rows :] + product[rows : 2 * rows] + product[:rows]


def ring_pairs(size, inner, step):
    block = size // inner
    return [
        (outer * inner + place, (outer + step) % block * inner + place)
        for outer in range(block)
        for place in range(inner)
    ]


def inner_pairs(size, inner, step):
    return [
        (outer * inner + place, outer * inner + (place + step) % inner)
        for outer in range(size // inner)
        for place in range(inner)
    ]


def send_z(value, step):
    return lax.ppermute(value, "dp", ring_pairs(Z_SIDE * X_SIDE, X_SIDE, step))


def send_x(value, step):
    return lax.ppermute(value, "dp", inner_pairs(Z_SIDE * X_SIDE, X_SIDE, step))


def send_y(value, step):
    return lax.ppermute(value, "fsdp", ring_pairs(Y_SIDE * CORES, CORES, step))


def swap_cores(value):
    return lax.ppermute(value, "fsdp", inner_pairs(Y_SIDE * CORES, CORES, 1))


def both_ways(value, send):
    return send(value, 1), send(value, -1)


def both_halves(before, after, send):
    half = before.shape[0] // 2
    return send(before[:half], 1), send(after[half:], -1)


def fence(*values):
    return lax.optimization_barrier(values)


def second_kernel(hidden_ref, *rest):
    sources = rest[: 2 * X_SIDE]
    kept_ref, sent_ref, blocks, flipped, arrived = rest[2 * X_SIDE :]
    core = lax.axis_index("fsdp") % CORES
    rows = blocks.shape[1]
    members = Z_SIDE // 2
    copies = [
        pltpu.make_async_copy(source, blocks.at[place], arrived.at[place])
        for place, source in enumerate(sources)
    ]
    for copy in copies:
        copy.start()
    flipped[...] = hidden_ref[...].T
    for place, copy in enumerate(copies):
        copy.wait()
        product = jnp.dot(blocks[place], flipped[...], preferred_element_type=jnp.float32)
        product = product.reshape(members, rows // members, -1)
        for pair in range(members // CORES):
            y = place % 2 * (members // CORES) + pair
            first, second = product[CORES * pair], product[CORES * pair + 1]
            kept_ref[y, place // 2] = jnp.where(core == 0, first, second).astype(jnp.bfloat16)
            sent_ref[y, place // 2] = jnp.where(core == 0, second, first).astype(jnp.bfloat16)


def second_products(hidden, *blocks):
    tokens, depth = hidden.shape
    rows = blocks[0].shape[0]
    part = jax.ShapeDtypeStruct(
        (Y_SIDE, X_SIDE, 2 * rows // Z_SIDE, tokens), jnp.bfloat16
    )
    whole = pl.BlockSpec(memory_space=pltpu.VMEM)
    apart = pl.BlockSpec(memory_space=pl.ANY)
    kept, sent = pl.pallas_call(
        second_kernel,
        out_shape=(part, part),
        in_specs=[whole] + [apart] * len(blocks),
        out_specs=(whole, whole),
        scratch_shapes=[
            pltpu.VMEM((8, rows, depth), jnp.bfloat16),
            pltpu.VMEM((depth, tokens), jnp.bfloat16),
            pltpu.SemaphoreType.DMA((8,)),
        ],
        compiler_params=pltpu.CompilerParams(vmem_limit_bytes=40 * 1024 * 1024),
        cost_estimate=pl.CostEstimate(
            flops=16 * rows * depth * tokens, bytes_accessed=20 * rows * depth, transcendentals=0
        ),
    )(hidden, *blocks)
    shape = (Y_SIDE, -1, tokens)
    return kept.reshape(shape), sent.reshape(shape)


def scatter_sums(kept, sent, y_index):
    received = swap_cores(sent)

    def both(step):
        place = (y_index + step) % Y_SIDE
        mine = lax.dynamic_index_in_dim(kept, place, 0, keepdims=False).astype(jnp.float32)
        return mine + lax.dynamic_index_in_dim(received, place, 0, keepdims=False)

    half = kept.shape[1] // 2
    far = both(2).astype(jnp.bfloat16)
    from_below = send_y(far[:half], 1)
    from_above = send_y(far[half:], -1)
    following = both(1)
    following = jnp.concatenate([following[:half] + from_below, following[half:]], 0)
    previous = both(3)
    previous = jnp.concatenate([previous[:half], previous[half:] + from_above], 0)
    below = send_y(following.astype(jnp.bfloat16), 1)
    above = send_y(previous.astype(jnp.bfloat16), -1)
    return both(0) + below + above


def on_device(
    incoming_feature_maps,
    spatial_filter_tensor,
    spatial_filter_offset,
    unit_layernorm_multiplier,
    unit_layernorm_offset_vector,
    expansion_linear_map,
    expansion_offset,
    contraction_linear_map,
    contraction_offset,
    residual_channel_factor,
    readout_layernorm_multiplier,
    readout_layernorm_offset,
    readout_linear_map,
    learner_caption_vectors,
    mentor_caption_vectors,
    mentor_picture_vectors,
    divisor_per_slot,
    active_program_slot,
    matching_caption_slot,
):
    group_count = incoming_feature_maps.shape[0]
    local_width = incoming_feature_maps.shape[3]
    shard_count = lax.axis_size("fsdp")
    shard_index = lax.axis_index("fsdp")
    data_index = lax.axis_index("dp")
    z_index = data_index // X_SIDE
    x_index = data_index % X_SIDE
    y_index = shard_index // CORES
    full_width = local_width * shard_count
    token_rows = group_count * SIDE * SIDE
    key_count = learner_caption_vectors.shape[0]
    second_rows = contraction_linear_map.shape[1]
    logit_divisor = lax.dynamic_index_in_dim(
        divisor_per_slot, active_program_slot[0], keepdims=False
    )

    own_x = lax.all_gather(
        contraction_linear_map.T, "dp", axis=0, tiled=True, axis_index_groups=Z_GROUPS
    )
    around = [send_x(expansion_linear_map, step) for step in (-1, 2, 1)]
    convolved = depthwise(incoming_feature_maps, spatial_filter_tensor, spatial_filter_offset)
    values = convolved.astype(jnp.float32).reshape(token_rows, local_width)
    sums = jnp.stack([jnp.sum(values, 1), jnp.sum(values * values, 1)])
    around, convolved, sums = fence(around, convolved, sums)

    def placed(buffer, part, step):
        return lax.dynamic_update_index_in_dim(buffer, part, (x_index + step) % X_SIDE, 0)

    block = jnp.zeros((X_SIDE,) + expansion_linear_map.shape, jnp.bfloat16)
    for step, part in enumerate([expansion_linear_map] + around):
        block = placed(block, part, step)
    first = {0: block.reshape(-1, block.shape[2])}
    first[7], first[1] = both_ways(first[0], send_z)
    totals, squares = jnp.sum(broadcast_gather(sums, "fsdp"), 0)
    mean_val = totals / full_width
    spread = squares / full_width - mean_val * mean_val
    gain_part = lax.dynamic_slice_in_dim(
        unit_layernorm_multiplier, shard_index * local_width, local_width
    )
    shift_part = lax.dynamic_slice_in_dim(
        unit_layernorm_offset_vector, shard_index * local_width, local_width
    )
    values = convolved.astype(jnp.float32).reshape(token_rows, local_width)
    local_normed = (
        (values - mean_val[:, None]) / jnp.sqrt(spread[:, None] + EPSILON) * gain_part + shift_part
    ).astype(jnp.bfloat16)
    head_rows = jnp.stack([readout_layernorm_multiplier, readout_layernorm_offset])
    head_rows = split_product(head_rows, readout_linear_map)
    teacher_rows = unit_rows(mentor_picture_vectors.astype(jnp.float32))
    own_keys = jnp.concatenate(
        [
            unit_rows(keys.astype(jnp.float32))
            for keys in (learner_caption_vectors, mentor_caption_vectors)
        ],
        1,
    )
    part_rows = own_x.shape[0] // 2
    own_low, own_high = own_x[:part_rows], own_x[part_rows:]
    first, head_rows, teacher_rows, own_keys, local_normed, own_low, own_high = fence(
        first, head_rows, teacher_rows, own_keys, local_normed, own_low, own_high
    )

    near_low = both_ways(own_low, send_x)
    first[6], first[2] = send_z(first[7], 1), send_z(first[1], -1)
    normed = lax.all_gather(local_normed, "fsdp", axis=0)
    first, near_low, own_keys = fence(first, near_low, own_keys)

    near_high = both_ways(own_high, send_x)
    far_low = send_x(near_low[0], 1)
    first[5], first[3] = send_z(first[6], 1), send_z(first[2], -1)
    all_keys = lax.all_gather(own_keys, "dp", axis=0, tiled=True)

    def first_product(place):
        part = lax.dynamic_index_in_dim(normed, (z_index + place) % Z_SIDE, 0, keepdims=False)
        return jnp.dot(part, first[place], preferred_element_type=jnp.float32)

    preact = first_product(0) + expansion_offset
    for place in (1, 7, 2, 6):
        preact = preact + first_product(place)
    first, near_high, preact = fence(first, near_high, preact)

    far_high = send_x(near_high[1], -1)
    step = both_halves(first[5], first[3], send_z)
    for place in (3, 5):
        preact = preact + first_product(place)
    step, preact, far_low, far_high = fence(step, preact, far_low, far_high)
    first[4] = jnp.concatenate(step, 0)
    preact = preact + first_product(4)
    hidden = jax.nn.gelu(preact, approximate=False).astype(jnp.bfloat16)

    blocks = (own_low, own_high, near_low[1], near_high[1], far_low, far_high)
    kept, sent = second_products(hidden, *blocks, near_low[0], near_high[0])
    branch = scatter_sums(kept, sent, y_index)
    branch = jnp.roll(branch.reshape(X_SIDE, second_rows, token_rows), x_index, 0)
    branch = branch.reshape(local_width, token_rows).T
    residual = incoming_feature_maps.astype(jnp.float32).reshape(token_rows, local_width)
    block_out = (
        (residual + residual_channel_factor * (branch + contraction_offset))
        .astype(jnp.bfloat16)
        .reshape(incoming_feature_maps.shape)
    )
    pooled = jnp.mean(
        block_out.astype(jnp.float32).reshape(group_count, SIDE * SIDE, local_width), 1
    )
    local_mean = jnp.mean(pooled, 1, keepdims=True)
    centered = pooled - local_mean
    local_square = jnp.sum(centered * centered, 1, keepdims=True)
    product = split_product(centered * readout_layernorm_multiplier, readout_linear_map)
    local_stats = jnp.concatenate([local_mean, local_square], 1).reshape(1, -1)
    local_stats = jnp.pad(local_stats, ((0, 0), (0, product.shape[1] - local_stats.shape[1])))
    shares = broadcast_gather(jnp.concatenate([product, head_rows, local_stats], 0), "fsdp")
    head_stats = shares[:, group_count + 2, : 2 * group_count].reshape(shard_count, group_count, 2)
    means, head_squares = head_stats[:, :, 0], head_stats[:, :, 1]
    mean_val = jnp.mean(means, 0)
    offsets = means - mean_val
    spread = jnp.sum(head_squares + local_width * (offsets * offsets), 0) / full_width
    scaled = jnp.sum(
        shares[:, :group_count] + offsets[:, :, None] * shares[:, group_count, None, :], 0
    )
    embedding = scaled / jnp.sqrt(spread[:, None] + EPSILON) + jnp.sum(shares[:, group_count + 1], 0)
    student_rows = unit_rows(embedding)
    width = student_rows.shape[1]
    teacher = logits(teacher_rows, all_keys[:, width:], logit_divisor)
    top_teacher = jnp.max(teacher, 1, keepdims=True)
    teacher_weights = jnp.exp(teacher - top_teacher)
    sum_teacher = jnp.sum(teacher_weights, 1)
    student = logits(student_rows, all_keys[:, :width], logit_divisor)
    local_columns = lax.iota(jnp.int32, student.shape[1])
    column_ids = (
        local_columns // key_count * shard_count + shard_index
    ) * key_count + local_columns % key_count
    labels = lax.dynamic_slice_in_dim(matching_caption_slot, data_index * group_count, group_count)
    top_student = jnp.max(student, 1, keepdims=True)
    sum_student = jnp.sum(jnp.exp(student - top_student), 1)
    label_score = jnp.sum(jnp.where(labels[:, None] == column_ids[None, :], student, 0.0), 1)
    cross_sum = jnp.sum(teacher_weights * (teacher - student), 1)
    stats = jnp.stack(
        [top_student[:, 0], sum_student, top_teacher[:, 0], sum_teacher, cross_sum, label_score], 1
    )
    per_device = group_count // shard_count
    stats = lax.all_to_all(stats.reshape(shard_count, per_device, 6), "fsdp", 0, 0)
    top_s, sum_s, top_t, sum_t, cross, label = [stats[:, :, member] for member in range(6)]
    best_s = jnp.max(top_s, 0)
    best_t = jnp.max(top_t, 0)
    scale_t = jnp.exp(top_t - best_t)
    total_t = jnp.sum(sum_t * scale_t, 0)
    log_student = best_s + jnp.log(jnp.sum(sum_s * jnp.exp(top_s - best_s), 0))
    losses = (
        jnp.sum(cross * scale_t, 0) / total_t
        - (best_t + jnp.log(total_t))
        + 2.0 * log_student
        - jnp.sum(label, 0)
    )
    return (block_out, embedding, losses)


def solution(mesh):
    placed = (
        P("dp", None, None, "fsdp"),
        P(None, None, "fsdp"),
        P("fsdp"),
        P(),
        P(),
        P("dp", "fsdp"),
        P("fsdp"),
        P("fsdp", "dp"),
        P("fsdp"),
        P("fsdp"),
        P("fsdp"),
        P("fsdp"),
        P("fsdp", None),
        P(("dp", "fsdp"), None),
        P(("dp", "fsdp"), None),
        P("dp", None),
        P(),
        P(),
        P(),
    )
    return jax.shard_map(
        on_device,
        mesh=mesh,
        in_specs=placed,
        out_specs=(P("dp", None, None, "fsdp"), P("dp", None), P(("dp", "fsdp"))),
        check_vma=False,
    )
```

profile of v0, /device:TPU:1, one launch (start us, length us, event | category | flops | bytes accessed | tf_op | source)
XLA Modules:
  0.0 262.4 jit_solution(18287674916472696606)
XLA Ops:
  7.3 3.4 %collective-permute-start = (bf16[96,1536]{1,0:T(8,128)(2,1)}, bf16[96,1536]{1,0:T(8,128)(2,1)S(1)}, u32[]{:S(2)}, u32[]{:S(2)}) collective-permute-start(bf16[96,1536]{1,0:T(8,128)(2,1)} %param.24), channel_id=1, source_target_pairs={{0,24},{8,0},{16,8},{24,16},{32,56},{40,32},{48,40},{56,48},{64,88... | collective-permute-start | bytes 884744 | tf_op jit(solution)/shard_map/ppermute | solution.py:90
  11.8 1.1 convert_reduce_fusion.49
  12.9 1.1 convert_reduce_fusion.50
  16.2 5.7 %convert_reduce_fusion = (f32[8,8,8]{2,1,0:T(8,128)S(1)}, f32[8,8,8]{2,1,0:T(8,128)S(1)}, bf16[8,8,8,384]{3,2,1,0:T(8,128)(2,1)S(1)}) fusion(f32[384]{0:T(512)} %param.21, f32[384]{0:T(512)S(1)} %get-tuple-element.127, f32[384]{0:T(512)S(1)} %get-tuple-element.128, f32[384]{0:T(512)S(1)} %get-tuple-element.81, f32[384]{0:T(512)S(1)} %get-tuple-element.82, ...), kind=kLoop, calls=%fused_computation.86 | loop fusion | flops 20249600 | bytes 1260544 | tf_op jit(solution)/shard_map/reduce_sum | solution.py:229
  24.5 1.2 broadcast_in_dim.27
  28.3 5.4 %all-to-all-start = ((f32[8,2,512]{2,1,0:T(2,128)}), f32[8,2,512]{2,1,0:T(2,128)S(1)}, u32[]{:S(2)}, u32[]{:S(2)}) async-start(f32[8,2,512]{2,1,0:T(2,128)} %broadcast_in_dim.32), calls=%async_computation | async-start | bytes 65536 | tf_op jit(solution)/shard_map/all_to_all | solution.py:55
  36.0 5.6 %collective-permute-start.3 = (bf16[384,1536]{1,0:T(8,128)(2,1)}, bf16[384,1536]{1,0:T(8,128)(2,1)}, u32[]{:S(2)}, u32[]{:S(2)}) collective-permute-start(bf16[384,1536]{1,0:T(8,128)(2,1)} %bitcast.5), channel_id=1, source_target_pairs={{0,224},{8,232},{16,240},{24,248},{32,0},{40,8},{48,16},{56,24},{6... | collective-permute-start | bytes 3538952 | tf_op jit(solution)/shard_map/ppermute | solution.py:86
  42.6 23.1 %all-gather.5.cloned.1.call-done = bf16[768,1536]{1,0:T(8,128)(2,1)} async-done(((bf16[96,1536]{1,0:T(8,128)(2,1)}), bf16[768,1536]{1,0:T(8,128)(2,1)}) %all-gather.5.cloned.1.call-update) | async-done | bytes 2359312 | tf_op jit(solution)/shard_map/all_gather | solution.py:223
  65.7 1.8 fusion.219
  67.5 10.5 %collective-permute-done.3 = bf16[384,1536]{1,0:T(8,128)(2,1)} collective-permute-done((bf16[384,1536]{1,0:T(8,128)(2,1)}, bf16[384,1536]{1,0:T(8,128)(2,1)}, u32[]{:S(2)}, u32[]{:S(2)}) %collective-permute-start.3) | collective-permute-done | bytes 1179680 | tf_op jit(solution)/shard_map/ppermute | solution.py:86
  79.1 2.2 collective-permute-start.5
  82.0 2.1 collective-permute-start.8
  84.1 22.5 %collective-permute-done.5 = bf16[384,1536]{1,0:T(8,128)(2,1)} collective-permute-done((bf16[384,1536]{1,0:T(8,128)(2,1)}, bf16[384,1536]{1,0:T(8,128)(2,1)}, u32[]{:S(2)}, u32[]{:S(2)}) %collective-permute-start.5) | collective-permute-done | bytes 1179680 | tf_op jit(solution)/shard_map/ppermute | solution.py:86
  106.5 2.0 collective-permute-start.12
  110.0 2.3 collective-permute-start.9
  112.6 2.5 fusion.147
  115.2 2.3 fusion.145
  117.4 2.3 fusion.151
  119.7 2.3 fusion.149
  121.9 4.0 %fusion.3 = f32[512,1536]{1,0:T(8,128)} fusion(f32[512,1536]{1,0:T(8,128)S(1)} %fusion.145, f32[512,1536]{1,0:T(8,128)S(1)} %fusion.147, f32[512,1536]{1,0:T(8,128)S(1)} %fusion.149, f32[512,1536]{1,0:T(8,128)S(1)} %fusion.151, bf16[384,1536]{1,0:T(8,128)(2,1)} %bitcast.5, f32[1536]{0:T(1024)S(1)} %copy-done.12, bf16[8,512,384]{2,1,0:T(8,128)(2,1)S(1)} %bitcast.135, ...), kind=kOutput, calls=%fused_computation.53 | convolution fusion | flops 607911936 | bytes 17309700 | tf_op jit(solution)/shard_map/dot_general | solution.py:281
  126.0 10.0 %collective-permute-done.11.rest_7_ = bf16[384,1536]{1,0:T(8,128)(2,1)} collective-permute-done((bf16[384,1536]{1,0:T(8,128)(2,1)S(1)}, bf16[384,1536]{1,0:T(8,128)(2,1)}, u32[]{:S(2)}, u32[]{:S(2)}) %collective-permute-start.11) | collective-permute-done | bytes 1179680 | tf_op jit(solution)/shard_map/ppermute | solution.py:90
  136.0 1.4 collective-permute-done.10
  137.4 2.8 %collective-permute-start.16 = (bf16[384,1536]{1,0:T(8,128)(2,1)}, bf16[384,1536]{1,0:T(8,128)(2,1)S(1)}, u32[]{:S(2)}, u32[]{:S(2)}) collective-permute-start(bf16[384,1536]{1,0:T(8,128)(2,1)} %collective-permute-done.12.rest_3_), channel_id=1, source_target_pairs={{0,24},{8,0},{16,8},{24,16},{32,56},{40,32},{48,40},{56,48},{64,88... | collective-permute-start | bytes 3538952 | tf_op jit(solution)/shard_map/ppermute | solution.py:90
  140.2 1.1 slice.504
  142.0 1.1 slice.505
  143.1 2.4 collective-permute-start.14
  145.5 2.4 fusion.143
  147.9 2.4 add_add_fusion
  150.3 12.8 %collective-permute-done.15.rest_4_ = bf16[384,1536]{1,0:T(8,128)(2,1)} collective-permute-done((bf16[384,1536]{1,0:T(8,128)(2,1)}, bf16[384,1536]{1,0:T(8,128)(2,1)}, u32[]{:S(2)}, u32[]{:S(2)}) %collective-permute-start.15) | collective-permute-done | bytes 1179680 | tf_op jit(solution)/shard_map/ppermute | solution.py:90
  163.2 2.3 fusion.24
  165.4 6.9 %fusion.6.hidden_ref = bf16[512,1536]{1,0:T(8,128)(2,1)S(1)} fusion(f32[512,1536]{1,0:T(8,128)S(1)} %add_add_fusion, f32[512,1536]{1,0:T(8,128)S(1)} %fusion.24), kind=kLoop, calls=%fused_computation.56 | loop fusion | flops 51904512 | bytes 7864320 | tf_op jit(solution)/shard_map/convert_element_type | solution.py:295
  172.4 1.3 copy-done.4
  173.7 8.6 %shard_map.202 = (bf16[4,4,96,512]{3,2,1,0:T(8,128)(2,1)S(1)}, bf16[4,4,96,512]{3,2,1,0:T(8,128)(2,1)}) custom-call(bf16[512,1536]{1,0:T(8,128)(2,1)S(1)} %fusion.6.hidden_ref, bf16[384,1536]{1,0:T(8,128)(2,1)S(1)} %copy-done.2, bf16[384,1536]{1,0:T(8,128)(2,1)S(1)} %get-tuple-element.52.rest_1_, bf16[384,1536]{1,0:T(8,128)(2,1)} %collective-permute-done.8.rest_2_, ...), custom_call_target="tpu_custom_call" | custom-call | flops 4831838208 | bytes 11796480 | tf_op jit(solution)/shard_map/pallas_call | solution.py:146
  182.3 5.0 %collective-permute-start.17 = (bf16[4,384,512]{2,1,0:T(8,128)(2,1)}, bf16[4,384,512]{2,1,0:T(8,128)(2,1)}, u32[]{:S(2)}, u32[]{:S(2)}) collective-permute-start(bf16[4,384,512]{2,1,0:T(8,128)(2,1)} %bitcast.20), channel_id=1, source_target_pairs={{0,1},{1,0},{2,3},{3,2},{4,5},{5,4},{6,7},{7,6},{8,9},{9,8},{10,11... | collective-permute-start | bytes 4718600 | tf_op jit(solution)/shard_map/ppermute | solution.py:98
  187.3 3.4 %collective-permute-done.17 = bf16[4,384,512]{2,1,0:T(8,128)(2,1)} collective-permute-done((bf16[4,384,512]{2,1,0:T(8,128)(2,1)}, bf16[4,384,512]{2,1,0:T(8,128)(2,1)}, u32[]{:S(2)}, u32[]{:S(2)}) %collective-permute-start.17) | collective-permute-done | bytes 1572896 | tf_op jit(solution)/shard_map/ppermute | solution.py:98
  190.7 1.5 convert_add_fusion.1
  192.6 2.5 collective-permute-start.20
  195.1 4.7 %collective-permute-done.18 = bf16[192,512]{1,0:T(8,128)(2,1)S(1)} collective-permute-done((bf16[192,512]{1,0:T(8,128)(2,1)S(1)}, bf16[192,512]{1,0:T(8,128)(2,1)S(1)}, u32[]{:S(2)}, u32[]{:S(2)}) %collective-permute-start.18) | collective-permute-done | bytes 196640 | tf_op jit(solution)/shard_map/ppermute | solution.py:94
  200.8 2.7 %collective-permute-start.21 = (bf16[384,512]{1,0:T(8,128)(2,1)}, bf16[384,512]{1,0:T(8,128)(2,1)S(1)}, u32[]{:S(2)}, u32[]{:S(2)}) collective-permute-start(bf16[384,512]{1,0:T(8,128)(2,1)} %pad_maximum_fusion.1), channel_id=1, source_target_pairs={{0,6},{1,7},{2,0},{3,1},{4,2},{5,3},{6,4},{7,5},{8,14},{9,15},{10,... | collective-permute-start | bytes 1179656 | tf_op jit(solution)/shard_map/ppermute | solution.py:94
  203.5 7.2 %collective-permute-done.19 = bf16[384,512]{1,0:T(8,128)(2,1)S(1)} collective-permute-done((bf16[384,512]{1,0:T(8,128)(2,1)S(1)}, bf16[384,512]{1,0:T(8,128)(2,1)S(1)}, u32[]{:S(2)}, u32[]{:S(2)}) %collective-permute-start.19) | collective-permute-done | bytes 393248 | tf_op jit(solution)/shard_map/ppermute | solution.py:94
  210.8 1.2 fusion.132
  212.5 1.9 convert_reduce_fusion.1
  215.9 7.2 %all-to-all-start.1 = ((f32[8,11,768]{2,1,0:T(8,128)}), f32[8,11,768]{2,1,0:T(8,128)S(1)}, u32[]{:S(2)}, u32[]{:S(2)}) async-start(f32[8,11,768]{2,1,0:T(8,128)} %broadcast_in_dim.34), calls=%async_computation.1 | async-start | bytes 786432 | tf_op jit(solution)/shard_map/all_to_all | solution.py:55
  224.5 6.7 %all-to-all-done.1 = f32[8,11,768]{2,1,0:T(8,128)S(1)} async-done(((f32[8,11,768]{2,1,0:T(8,128)}), f32[8,11,768]{2,1,0:T(8,128)S(1)}, u32[]{:S(2)}, u32[]{:S(2)}) %all-to-all-start.1) | async-done | bytes 270368 | tf_op jit(solution)/shard_map/all_to_all | solution.py:55
  232.0 3.6 %fusion.223 = (f32[8]{0:T(128)S(1)}, f32[8,2048]{1,0:T(8,128)S(1)}) fusion(f32[]{:T(128)} %bitcast.40, bf16[8,768]{1,0:T(8,128)(2,1)S(1)} %fusion.171, bf16[2048,1536]{1,0:T(8,128)(2,1)} %all-gather.7.cloned.1.call-done), kind=kOutput, calls=%fused_computation.407 | convolution fusion | flops 25198584 | bytes 3224096 | tf_op jit(solution)/shard_map/dot_general | solution.py:46
  235.6 3.6 %fusion.222 = (f32[8]{0:T(128)S(1)}, f32[8,2048]{1,0:T(8,128)S(1)}) fusion(f32[]{:T(128)} %bitcast.40, bf16[2048,1536]{1,0:T(8,128)(2,1)} %all-gather.7.cloned.1.call-done, f32[8,768]{1,0:T(8,128)S(1)} %get-tuple-element.136, f32[8]{0:T(128)S(1)} %add_sqrt_fusion.1), kind=kOutput, calls=%fused_computation.406 | convolution fusion | flops 25210872 | bytes 3236416 | tf_op jit(solution)/shard_map/dot_general | solution.py:46
  239.5 7.8 %all_to_all.15 = f32[8,1,6]{2,1,0:T(1,128)S(1)} all-to-all(f32[8,1,6]{2,1,0:T(1,128)S(1)} %copy.76), channel_id=1, replica_groups=mesh['dp'=32,'fsdp'=8] {'fsdp'}, dimensions={0} | all-to-all | bytes 384 | tf_op jit(solution)/shard_map/all_to_all | solution.py:347
  248.1 2.1 slice_reduce_fusion.1
  (141 shorter events, 21.8 us)
Async XLA Ops:
  7.2 17.0 %copy-start = (bf16[384,768]{1,0:T(8,128)(2,1)S(1)}, bf16[384,768]{1,0:T(8,128)(2,1)}, u32[]{:S(2)}) copy-start(bf16[384,768]{1,0:T(8,128)(2,1)} %param.31) | copy-start | bytes 1769476
  7.2 18.5 %copy-start.9 = (bf16[96,1536]{1,0:T(8,128)(2,1)S(1)}, bf16[96,1536]{1,0:T(8,128)(2,1)}, u32[]{:S(2)}) copy-start(bf16[96,1536]{1,0:T(8,128)(2,1)} %param.24) | copy-start | bytes 884740
  7.2 16.4 %copy-start.13 = (f32[384]{0:T(512)S(1)}, f32[384]{0:T(512)}, u32[]{:S(2)}) copy-start(f32[384]{0:T(512)} %param.29) | copy-start | bytes 4612
  7.2 16.4 %copy-start.16 = (f32[384]{0:T(512)S(1)}, f32[384]{0:T(512)}, u32[]{:S(2)}) copy-start(f32[384]{0:T(512)} %param.30) | copy-start | bytes 4612
  7.2 16.4 %copy-start.8 = (bf16[64,768]{1,0:T(8,128)(2,1)S(1)}, bf16[64,768]{1,0:T(8,128)(2,1)}, u32[]{:S(2)}) copy-start(bf16[64,768]{1,0:T(8,128)(2,1)} %param.33) | copy-start | bytes 294916
  7.2 16.5 %copy-start.7 = (bf16[64,768]{1,0:T(8,128)(2,1)S(1)}, bf16[64,768]{1,0:T(8,128)(2,1)}, u32[]{:S(2)}) copy-start(bf16[64,768]{1,0:T(8,128)(2,1)} %param.32) | copy-start | bytes 294916
  7.2 16.6 %copy-start.10 = (bf16[8,768]{1,0:T(8,128)(2,1)S(1)}, bf16[8,768]{1,0:T(8,128)(2,1)}, u32[]{:S(2)}) copy-start(bf16[8,768]{1,0:T(8,128)(2,1)} %param.34) | copy-start | bytes 36868
  7.2 58.5 %all-gather.5.cloned.1.call-start = ((), (), s32[]{:S(2)}) async-start(), calls=%async_computation.3 | async-start | bytes 2654208 | tf_op jit(solution)/shard_map/all_gather | solution.py:223
  7.3 19.8 %collective-permute-start = (bf16[96,1536]{1,0:T(8,128)(2,1)}, bf16[96,1536]{1,0:T(8,128)(2,1)S(1)}, u32[]{:S(2)}, u32[]{:S(2)}) collective-permute-start(bf16[96,1536]{1,0:T(8,128)(2,1)} %param.24), channel_id=1, source_target_pairs={{0,24},{8,0},{16,8},{24,16},{32,56},{40,32},{48,40},{56,48},{64,88... | collective-permute-start | bytes 884744 | tf_op jit(solution)/shard_map/ppermute | solution.py:90
  10.7 16.4 %collective-permute-start.1 = (bf16[96,1536]{1,0:T(8,128)(2,1)}, bf16[96,1536]{1,0:T(8,128)(2,1)S(1)}, u32[]{:S(2)}, u32[]{:S(2)}) collective-permute-start(bf16[96,1536]{1,0:T(8,128)(2,1)} %param.24), channel_id=1, source_target_pairs={{0,16},{8,24},{16,0},{24,8},{32,48},{40,56},{48,32},{56,40},{64,80... | collective-permute-start | bytes 884744 | tf_op jit(solution)/shard_map/ppermute | solution.py:90
  11.2 16.4 %collective-permute-start.2 = (bf16[96,1536]{1,0:T(8,128)(2,1)}, bf16[96,1536]{1,0:T(8,128)(2,1)S(1)}, u32[]{:S(2)}, u32[]{:S(2)}) collective-permute-start(bf16[96,1536]{1,0:T(8,128)(2,1)} %param.24), channel_id=1, source_target_pairs={{0,8},{8,16},{16,24},{24,0},{32,40},{40,48},{48,56},{56,32},{64,72... | collective-permute-start | bytes 884744 | tf_op jit(solution)/shard_map/ppermute | solution.py:90
  28.3 13.3 %all-to-all-start = ((f32[8,2,512]{2,1,0:T(2,128)}), f32[8,2,512]{2,1,0:T(2,128)S(1)}, u32[]{:S(2)}, u32[]{:S(2)}) async-start(f32[8,2,512]{2,1,0:T(2,128)} %broadcast_in_dim.32), calls=%async_computation | async-start | bytes 65536 | tf_op jit(solution)/shard_map/all_to_all | solution.py:55
  33.7 78.9 %all-gather.9.cloned.1.call-start = ((), (), s32[]{:S(2)}) async-start(), calls=%async_computation.5 | async-start | bytes 3538944 | tf_op jit(solution)/shard_map/all_gather | solution.py:271
  36.0 42.0 %collective-permute-start.3 = (bf16[384,1536]{1,0:T(8,128)(2,1)}, bf16[384,1536]{1,0:T(8,128)(2,1)}, u32[]{:S(2)}, u32[]{:S(2)}) collective-permute-start(bf16[384,1536]{1,0:T(8,128)(2,1)} %bitcast.5), channel_id=1, source_target_pairs={{0,224},{8,232},{16,240},{24,248},{32,0},{40,8},{48,16},{56,24},{6... | collective-permute-start | bytes 3538952 | tf_op jit(solution)/shard_map/ppermute | solution.py:86
  41.5 37.5 %collective-permute-start.4 = (bf16[384,1536]{1,0:T(8,128)(2,1)}, bf16[384,1536]{1,0:T(8,128)(2,1)}, u32[]{:S(2)}, u32[]{:S(2)}) collective-permute-start(bf16[384,1536]{1,0:T(8,128)(2,1)} %bitcast.5), channel_id=1, source_target_pairs={{0,32},{8,40},{16,48},{24,56},{32,64},{40,72},{48,80},{56,88},{64,... | collective-permute-start | bytes 3538952 | tf_op jit(solution)/shard_map/ppermute | solution.py:86
  67.5 47.7 %copy-start.1 = (bf16[384,1536]{1,0:T(8,128)(2,1)}, bf16[384,1536]{1,0:T(8,128)(2,1)S(1)}, u32[]{:S(2)}) copy-start(bf16[384,1536]{1,0:T(8,128)(2,1)S(1)} %get-tuple-element.45.rest_0_) | copy-start | bytes 3538948
  79.1 152.9 %all-gather.7.cloned.1.call-start = ((), (), s32[]{:S(2)}) async-start(), calls=%async_computation.4 | async-start | bytes 6488064 | tf_op jit(solution)/shard_map/all_gather | solution.py:277
  79.1 27.4 %collective-permute-start.5 = (bf16[384,1536]{1,0:T(8,128)(2,1)}, bf16[384,1536]{1,0:T(8,128)(2,1)}, u32[]{:S(2)}, u32[]{:S(2)}) collective-permute-start(bf16[384,1536]{1,0:T(8,128)(2,1)} %collective-permute-done.3), channel_id=1, source_target_pairs={{0,224},{8,232},{16,240},{24,248},{32,0},{40,8},{48,16},{56,24},{6... | collective-permute-start | bytes 3538952 | tf_op jit(solution)/shard_map/ppermute | solution.py:86
  81.4 28.2 %collective-permute-start.6 = (bf16[384,1536]{1,0:T(8,128)(2,1)}, bf16[384,1536]{1,0:T(8,128)(2,1)}, u32[]{:S(2)}, u32[]{:S(2)}) collective-permute-start(bf16[384,1536]{1,0:T(8,128)(2,1)} %collective-permute-done.4), channel_id=1, source_target_pairs={{0,32},{8,40},{16,48},{24,56},{32,64},{40,72},{48,80},{56,88},{64,... | collective-permute-start | bytes 3538952 | tf_op jit(solution)/shard_map/ppermute | solution.py:86
  81.4 28.2 %collective-permute-start.7 = (bf16[384,1536]{1,0:T(8,128)(2,1)S(1)}, bf16[384,1536]{1,0:T(8,128)(2,1)}, u32[]{:S(2)}, u32[]{:S(2)}) collective-permute-start(bf16[384,1536]{1,0:T(8,128)(2,1)S(1)} %get-tuple-element.45.rest_0_), channel_id=1, source_target_pairs={{0,8},{8,16},{16,24},{24,0},{32,40},{40,48},{48,56},{56,32},{64,72... | collective-permute-start | bytes 3538952 | tf_op jit(solution)/shard_map/ppermute | solution.py:90
  82.0 27.6 %collective-permute-start.8 = (bf16[384,1536]{1,0:T(8,128)(2,1)S(1)}, bf16[384,1536]{1,0:T(8,128)(2,1)}, u32[]{:S(2)}, u32[]{:S(2)}) collective-permute-start(bf16[384,1536]{1,0:T(8,128)(2,1)S(1)} %get-tuple-element.45.rest_0_), channel_id=1, source_target_pairs={{0,24},{8,0},{16,8},{24,16},{32,56},{40,32},{48,40},{56,48},{64,88... | collective-permute-start | bytes 3538952 | tf_op jit(solution)/shard_map/ppermute | solution.py:90
  84.1 52.0 %collective-permute-start.11 = (bf16[384,1536]{1,0:T(8,128)(2,1)S(1)}, bf16[384,1536]{1,0:T(8,128)(2,1)}, u32[]{:S(2)}, u32[]{:S(2)}) collective-permute-start(bf16[384,1536]{1,0:T(8,128)(2,1)S(1)} %get-tuple-element.52.rest_1_), channel_id=1, source_target_pairs={{0,8},{8,16},{16,24},{24,0},{32,40},{40,48},{48,56},{56,32},{64,72... | collective-permute-start | bytes 3538952 | tf_op jit(solution)/shard_map/ppermute | solution.py:90
  106.5 29.5 %collective-permute-start.12 = (bf16[384,1536]{1,0:T(8,128)(2,1)S(1)}, bf16[384,1536]{1,0:T(8,128)(2,1)}, u32[]{:S(2)}, u32[]{:S(2)}) collective-permute-start(bf16[384,1536]{1,0:T(8,128)(2,1)S(1)} %get-tuple-element.52.rest_1_), channel_id=1, source_target_pairs={{0,24},{8,0},{16,8},{24,16},{32,56},{40,32},{48,40},{56,48},{64,88... | collective-permute-start | bytes 3538952 | tf_op jit(solution)/shard_map/ppermute | solution.py:90
  109.6 27.8 %collective-permute-start.10 = (bf16[384,1536]{1,0:T(8,128)(2,1)}, bf16[384,1536]{1,0:T(8,128)(2,1)}, u32[]{:S(2)}, u32[]{:S(2)}) collective-permute-start(bf16[384,1536]{1,0:T(8,128)(2,1)} %collective-permute-done.6), channel_id=1, source_target_pairs={{0,32},{8,40},{16,48},{24,56},{32,64},{40,72},{48,80},{56,88},{64,... | collective-permute-start | bytes 3538952 | tf_op jit(solution)/shard_map/ppermute | solution.py:86
  110.0 27.4 %collective-permute-start.9 = (bf16[384,1536]{1,0:T(8,128)(2,1)}, bf16[384,1536]{1,0:T(8,128)(2,1)}, u32[]{:S(2)}, u32[]{:S(2)}) collective-permute-start(bf16[384,1536]{1,0:T(8,128)(2,1)} %collective-permute-done.5), channel_id=1, source_target_pairs={{0,224},{8,232},{16,240},{24,248},{32,0},{40,8},{48,16},{56,24},{6... | collective-permute-start | bytes 3538952 | tf_op jit(solution)/shard_map/ppermute | solution.py:86
  112.3 50.8 %collective-permute-start.15 = (bf16[384,1536]{1,0:T(8,128)(2,1)}, bf16[384,1536]{1,0:T(8,128)(2,1)}, u32[]{:S(2)}, u32[]{:S(2)}) collective-permute-start(bf16[384,1536]{1,0:T(8,128)(2,1)} %collective-permute-done.7.rest_6_), channel_id=1, source_target_pairs={{0,8},{8,16},{16,24},{24,0},{32,40},{40,48},{48,56},{56,32},{64,72... | collective-permute-start | bytes 3538952 | tf_op jit(solution)/shard_map/ppermute | solution.py:90
  112.6 2.5 copy-start.6
  119.7 2.3 copy-start.12
  137.4 25.7 %collective-permute-start.16 = (bf16[384,1536]{1,0:T(8,128)(2,1)}, bf16[384,1536]{1,0:T(8,128)(2,1)S(1)}, u32[]{:S(2)}, u32[]{:S(2)}) collective-permute-start(bf16[384,1536]{1,0:T(8,128)(2,1)} %collective-permute-done.12.rest_3_), channel_id=1, source_target_pairs={{0,24},{8,0},{16,8},{24,16},{32,56},{40,32},{48,40},{56,48},{64,88... | collective-permute-start | bytes 3538952 | tf_op jit(solution)/shard_map/ppermute | solution.py:90
  141.3 21.8 %collective-permute-start.13 = (bf16[192,1536]{1,0:T(8,128)(2,1)S(1)}, bf16[192,1536]{1,0:T(8,128)(2,1)S(1)}, u32[]{:S(2)}, u32[]{:S(2)}) collective-permute-start(bf16[192,1536]{1,0:T(8,128)(2,1)S(1)} %slice.504), channel_id=1, source_target_pairs={{0,32},{8,40},{16,48},{24,56},{32,64},{40,72},{48,80},{56,88},{64,... | collective-permute-start | bytes 1769480 | tf_op jit(solution)/shard_map/ppermute | solution.py:86
  143.1 4.8 %copy-start.5 = (f32[512,1536]{1,0:T(8,128)S(1)}, f32[512,1536]{1,0:T(8,128)}, u32[]{:S(2)}) copy-start(f32[512,1536]{1,0:T(8,128)} %fusion.3) | copy-start | bytes 9437188
  143.1 20.1 %collective-permute-start.14 = (bf16[192,1536]{1,0:T(8,128)(2,1)S(1)}, bf16[192,1536]{1,0:T(8,128)(2,1)S(1)}, u32[]{:S(2)}, u32[]{:S(2)}) collective-permute-start(bf16[192,1536]{1,0:T(8,128)(2,1)S(1)} %slice.505), channel_id=1, source_target_pairs={{0,224},{8,232},{16,240},{24,248},{32,0},{40,8},{48,16},{56,24},{6... | collective-permute-start | bytes 1769480 | tf_op jit(solution)/shard_map/ppermute | solution.py:86
  163.2 2.3 copy-start.3
  165.4 6.9 %copy-start.2 = (bf16[384,1536]{1,0:T(8,128)(2,1)S(1)}, bf16[384,1536]{1,0:T(8,128)(2,1)}, u32[]{:S(2)}) copy-start(bf16[384,1536]{1,0:T(8,128)(2,1)} %copy-done.1) | copy-start | bytes 3538948
  172.4 1.3 copy-start.4
  182.3 8.4 %collective-permute-start.17 = (bf16[4,384,512]{2,1,0:T(8,128)(2,1)}, bf16[4,384,512]{2,1,0:T(8,128)(2,1)}, u32[]{:S(2)}, u32[]{:S(2)}) collective-permute-start(bf16[4,384,512]{2,1,0:T(8,128)(2,1)} %bitcast.20), channel_id=1, source_target_pairs={{0,1},{1,0},{2,3},{3,2},{4,5},{5,4},{6,7},{7,6},{8,9},{9,8},{10,11... | collective-permute-start | bytes 4718600 | tf_op jit(solution)/shard_map/ppermute | solution.py:98
  192.3 7.5 %collective-permute-start.18 = (bf16[192,512]{1,0:T(8,128)(2,1)S(1)}, bf16[192,512]{1,0:T(8,128)(2,1)S(1)}, u32[]{:S(2)}, u32[]{:S(2)}) collective-permute-start(bf16[192,512]{1,0:T(8,128)(2,1)S(1)} %get-tuple-element.147), channel_id=1, source_target_pairs={{0,2},{1,3},{2,4},{3,5},{4,6},{5,7},{6,0},{7,1},{8,10},{9,11},{10,... | collective-permute-start | bytes 589832 | tf_op jit(solution)/shard_map/ppermute | solution.py:94
  192.6 7.4 %collective-permute-start.20 = (bf16[192,512]{1,0:T(8,128)(2,1)S(1)}, bf16[192,512]{1,0:T(8,128)(2,1)S(1)}, u32[]{:S(2)}, u32[]{:S(2)}) collective-permute-start(bf16[192,512]{1,0:T(8,128)(2,1)S(1)} %get-tuple-element.148), channel_id=1, source_target_pairs={{0,6},{1,7},{2,0},{3,1},{4,2},{5,3},{6,4},{7,5},{8,14},{9,15},{10,... | collective-permute-start | bytes 589832 | tf_op jit(solution)/shard_map/ppermute | solution.py:94
  199.9 10.8 %collective-permute-start.19 = (bf16[384,512]{1,0:T(8,128)(2,1)S(1)}, bf16[384,512]{1,0:T(8,128)(2,1)S(1)}, u32[]{:S(2)}, u32[]{:S(2)}) collective-permute-start(bf16[384,512]{1,0:T(8,128)(2,1)S(1)} %pad_maximum_fusion), channel_id=1, source_target_pairs={{0,2},{1,3},{2,4},{3,5},{4,6},{5,7},{6,0},{7,1},{8,10},{9,11},{10,... | collective-permute-start | bytes 1179656 | tf_op jit(solution)/shard_map/ppermute | solution.py:94
  200.0 12.5 %copy-start.14 = (f32[384]{0:T(512)S(1)}, f32[384]{0:T(512)}, u32[]{:S(2)}) copy-start(f32[384]{0:T(512)} %param.27) | copy-start | bytes 4612
  200.0 12.5 %copy-start.15 = (f32[384]{0:T(512)S(1)}, f32[384]{0:T(512)}, u32[]{:S(2)}) copy-start(f32[384]{0:T(512)} %param.28) | copy-start | bytes 4612
  200.8 10.0 %collective-permute-start.21 = (bf16[384,512]{1,0:T(8,128)(2,1)}, bf16[384,512]{1,0:T(8,128)(2,1)S(1)}, u32[]{:S(2)}, u32[]{:S(2)}) collective-permute-start(bf16[384,512]{1,0:T(8,128)(2,1)} %pad_maximum_fusion.1), channel_id=1, source_target_pairs={{0,6},{1,7},{2,0},{3,1},{4,2},{5,3},{6,4},{7,5},{8,14},{9,15},{10,... | collective-permute-start | bytes 1179656 | tf_op jit(solution)/shard_map/ppermute | solution.py:94
  212.0 11.8 %copy-start.18 = (f32[64]{0:T(128)S(1)}, f32[64]{0:T(128)}, u32[]{:S(2)}) copy-start(f32[64]{0:T(128)} %param.35) | copy-start | bytes 772
  212.0 12.4 %copy-start.17 = (s32[256]{0:T(256)S(1)}, s32[256]{0:T(256)}, u32[]{:S(2)}) copy-start(s32[256]{0:T(256)} %param.37) | copy-start | bytes 3076
  215.9 15.3 %all-to-all-start.1 = ((f32[8,11,768]{2,1,0:T(8,128)}), f32[8,11,768]{2,1,0:T(8,128)S(1)}, u32[]{:S(2)}, u32[]{:S(2)}) async-start(f32[8,11,768]{2,1,0:T(8,128)} %broadcast_in_dim.34), calls=%async_computation.1 | async-start | bytes 786432 | tf_op jit(solution)/shard_map/all_to_all | solution.py:55
  232.0 7.2 %copy-start.11 = (f32[8,768]{1,0:T(8,128)}, f32[8,768]{1,0:T(8,128)S(1)}, u32[]{:S(2)}) copy-start(f32[8,768]{1,0:T(8,128)S(1)} %get-tuple-element.136) | copy-start | bytes 73732
Sparse Core Ops, SparseCore 0:
  11.9 53.7 all-gather.4
  79.2 29.0 all-gather.8
  112.7 91.4 all-gather.6
where the time goes:
time: 264 us; the launch traced here: 262 us
  waiting for transfers between devices  105 us (40%)
  starting transfers between devices  49 us (19%)
  other arithmetic  28.9 us (11%)
  matrix products  27.9 us (11%)
  between operations  20.7 us (8%)
  local copies, waits for them, and re-layouts  14.2 us (5%)
  Pallas kernels  8.61 us (3%)
  blocking collectives  7.79 us (3%)
    ppermute x8, waiting for transfers between devices, send_z(): return lax.ppermute(value, 'dp', ring_pairs(Z_SIDE * X_SIDE, X_SIDE, step))  36.5 us
    ppermute x9, waiting for transfers between devices, send_x(): return lax.ppermute(value, 'dp', inner_pairs(Z_SIDE * X_SIDE, X_SIDE, step))  23.4 us
    all_gather x1, waiting for transfers between devices, on_device(): lax.all_gather(contraction_linear_map.T, 'dp', axis=0, tiled=True, axis_i...  23.1 us
    dot_general x8, matrix products, first_product(): return jnp.dot(part, first[place], preferred_element_type=jnp.float32)  20.4 us
    ppermute x8, starting transfers between devices, send_z(): return lax.ppermute(value, 'dp', ring_pairs(Z_SIDE * X_SIDE, X_SIDE, step))  13.6 us
    all_to_all x2, starting transfers between devices, broadcast_gather(): return lax.all_to_all(copies, axis, 0, 0)  12.6 us
    ppermute x9, starting transfers between devices, send_x(): return lax.ppermute(value, 'dp', inner_pairs(Z_SIDE * X_SIDE, X_SIDE, step))  12.2 us
    ppermute x4, waiting for transfers between devices, send_y(): return lax.ppermute(value, 'fsdp', ring_pairs(Y_SIDE * CORES, CORES, step))  12 us
  transfers between devices with their start and end apart: 27, of which 14 were waited for; matrix products, arithmetic and copies ran while one was open for 23% of the time, Pallas kernels for 3%

commit v1 on v0

--- a/solution.py
+++ b/solution.py
@@ -11,6 +11,8 @@
 X_SIDE = 4
 Y_SIDE = 4
 CORES = 2
+TOKEN_TILE = 128
+SQRT_HALF = 0.5**0.5
 X_GROUPS = [[z * X_SIDE + x for x in range(X_SIDE)] for z in range(Z_SIDE)]
 Z_GROUPS = [[z * X_SIDE + x for z in range(Z_SIDE)] for x in range(X_SIDE)]
 
@@ -111,19 +113,35 @@
     return lax.optimization_barrier(values)
 
 
-def second_kernel(hidden_ref, *rest):
+def second_kernel(preact_ref, part_ref, low_ref, high_ref, *rest):
     sources = rest[: 2 * X_SIDE]
-    kept_ref, sent_ref, blocks, flipped, arrived = rest[2 * X_SIDE :]
+    kept_ref, sent_ref, last, blocks, flipped, arrived = rest[2 * X_SIDE :]
     core = lax.axis_index("fsdp") % CORES
+    depth = low_ref.shape[0]
+    tokens = preact_ref.shape[0]
     rows = blocks.shape[1]
     members = Z_SIDE // 2
+    halves = [
+        pltpu.make_async_copy(
+            source, last.at[pl.ds(place * depth, depth)], arrived.at[len(sources) + place]
+        )
+        for place, source in enumerate((low_ref, high_ref))
+    ]
     copies = [
         pltpu.make_async_copy(source, blocks.at[place], arrived.at[place])
         for place, source in enumerate(sources)
     ]
-    for copy in copies:
+    for copy in halves + copies:
         copy.start()
-    flipped[...] = hidden_ref[...].T
+    for copy in halves:
+        copy.wait()
+    for start in range(0, tokens, TOKEN_TILE):
+        tile = pl.ds(start, TOKEN_TILE)
+        preact = preact_ref[tile, :] + jnp.dot(
+            part_ref[tile, :], last[...], preferred_element_type=jnp.float32
+        )
+        hidden = preact * (1.0 + lax.erf(preact * SQRT_HALF)) * 0.5
+        flipped[:, tile] = hidden.astype(jnp.bfloat16).T
     for place, copy in enumerate(copies):
         copy.wait()
         product = jnp.dot(blocks[place], flipped[...], preferred_element_type=jnp.float32)
@@ -135,29 +153,30 @@
             sent_ref[y, place // 2] = jnp.where(core == 0, second, first).astype(jnp.bfloat16)
 
 
-def second_products(hidden, *blocks):
-    tokens, depth = hidden.shape
+def second_products(preact, part, low, high, *blocks):
+    tokens, depth = preact.shape
     rows = blocks[0].shape[0]
-    part = jax.ShapeDtypeStruct(
+    shape = jax.ShapeDtypeStruct(
         (Y_SIDE, X_SIDE, 2 * rows // Z_SIDE, tokens), jnp.bfloat16
     )
     whole = pl.BlockSpec(memory_space=pltpu.VMEM)
     apart = pl.BlockSpec(memory_space=pl.ANY)
     kept, sent = pl.pallas_call(
         second_kernel,
-        out_shape=(part, part),
-        in_specs=[whole] + [apart] * len(blocks),
+        out_shape=(shape, shape),
+        in_specs=[whole] * 2 + [apart] * (2 + len(blocks)),
         out_specs=(whole, whole),
         scratch_shapes=[
+            pltpu.VMEM((2 * low.shape[0], depth), jnp.bfloat16),
             pltpu.VMEM((8, rows, depth), jnp.bfloat16),
             pltpu.VMEM((depth, tokens), jnp.bfloat16),
-            pltpu.SemaphoreType.DMA((8,)),
+            pltpu.SemaphoreType.DMA((10,)),
         ],
-        compiler_params=pltpu.CompilerParams(vmem_limit_bytes=40 * 1024 * 1024),
+        compiler_params=pltpu.CompilerParams(vmem_limit_bytes=44 * 1024 * 1024),
         cost_estimate=pl.CostEstimate(
             flops=16 * rows * depth * tokens, bytes_accessed=20 * rows * depth, transcendentals=0
         ),
-    )(hidden, *blocks)
+    )(preact, part, low, high, *blocks)
     shape = (Y_SIDE, -1, tokens)
     return kept.reshape(shape), sent.reshape(shape)
 
@@ -276,9 +295,11 @@
     first[5], first[3] = send_z(first[6], 1), send_z(first[2], -1)
     all_keys = lax.all_gather(own_keys, "dp", axis=0, tiled=True)
 
+    def part_of(place):
+        return lax.dynamic_index_in_dim(normed, (z_index + place) % Z_SIDE, 0, keepdims=False)
+
     def first_product(place):
-        part = lax.dynamic_index_in_dim(normed, (z_index + place) % Z_SIDE, 0, keepdims=False)
-        return jnp.dot(part, first[place], preferred_element_type=jnp.float32)
+        return jnp.dot(part_of(place), first[place], preferred_element_type=jnp.float32)
 
     preact = first_product(0) + expansion_offset
     for place in (1, 7, 2, 6):
@@ -289,13 +310,10 @@
     step = both_halves(first[5], first[3], send_z)
     for place in (3, 5):
         preact = preact + first_product(place)
-    step, preact, far_low, far_high = fence(step, preact, far_low, far_high)
-    first[4] = jnp.concatenate(step, 0)
-    preact = preact + first_product(4)
-    hidden = jax.nn.gelu(preact, approximate=False).astype(jnp.bfloat16)
-
+    last_part = part_of(4)
+    step, preact, far_low, far_high, last_part = fence(step, preact, far_low, far_high, last_part)
     blocks = (own_low, own_high, near_low[1], near_high[1], far_low, far_high)
-    kept, sent = second_products(hidden, *blocks, near_low[0], near_high[0])
+    kept, sent = second_products(preact, last_part, *step, *blocks, near_low[0], near_high[0])
     branch = scatter_sums(kept, sent, y_index)
     branch = jnp.roll(branch.reshape(X_SIDE, second_rows, token_rows), x_index, 0)
     branch = branch.reshape(local_width, token_rows).T
@@ -326,7 +344,7 @@
     embedding = scaled / jnp.sqrt(spread[:, None] + EPSILON) + jnp.sum(shares[:, group_count + 1], 0)
     student_rows = unit_rows(embedding)
     width = student_rows.shape[1]
-    teacher = logits(teacher_rows, all_keys[:, width:], logit_divisor)
+    teacher = logits(teacher_rows, all_keys[:, teacher_rows.shape[1] :], logit_divisor)
     top_teacher = jnp.max(teacher, 1, keepdims=True)
     teacher_weights = jnp.exp(teacher - top_teacher)
     sum_teacher = jnp.sum(teacher_weights, 1)

time: 264 us -> 277 us (1.049)
  starting transfers between devices: 49 us -> 59.8 us
  other arithmetic: 28.9 us -> 20.3 us
  waiting for transfers between devices: 105 us -> 111 us
  Pallas kernels: 8.61 us -> 12.4 us
  local copies, waits for them, and re-layouts: 14.2 us -> 17.6 us
    ppermute x1, starting transfers between devices: 5.04 us -> 17 us  [swap_cores(): return lax.ppermute(value, 'fsdp', inner_pairs(Y_SIDE * CORES, CORES, 1))]
    convert_element_type x1 -> x0, other arithmetic: 6.9 us -> none  [on_device(): hidden = jax.nn.gelu(preact, approximate=False).astype(jnp.bfloat16)]
    ppermute x8, waiting for transfers between devices: 36.5 us -> 40.8 us  [send_z(): return lax.ppermute(value, 'dp', ring_pairs(Z_SIDE * X_SIDE, X_SIDE, step))]
    pallas_call x1, Pallas kernels: 8.61 us -> 12.4 us  [second_products(): pl.pallas_call(second_kernel, out_shape=(shape, shape), in_specs=[whole]...]
    dot_general x8 -> x7, matrix products: 20.4 us -> 18.7 us  [first_product(): jnp.dot(part_of(place), first[place], preferred_element_type=jnp.float32)]
  transfers between devices with their start and end apart: 27 -> 27, of which waited for: 14 -> 16; matrix products, arithmetic and copies ran while one was open for 23% -> 18% of each run, Pallas kernels for 3% -> 4%
where the time goes in v1:
time: 277 us; the launch traced here: 276 us
  waiting for transfers between devices  111 us (40%)
  starting transfers between devices  59.8 us (22%)
  matrix products  26.2 us (9%)
  between operations  20.8 us (8%)
  other arithmetic  20.3 us (7%)
  local copies, waits for them, and re-layouts  17.6 us (6%)
  Pallas kernels  12.4 us (4%)
  blocking collectives  7.79 us (3%)
    ppermute x8, waiting for transfers between devices, send_z(): return lax.ppermute(value, 'dp', ring_pairs(Z_SIDE * X_SIDE, X_SIDE, step))  40.8 us
    ppermute x9, waiting for transfers between devices, send_x(): return lax.ppermute(value, 'dp', inner_pairs(Z_SIDE * X_SIDE, X_SIDE, step))  24.2 us
    all_gather x1, waiting for transfers between devices, on_device(): lax.all_gather(contraction_linear_map.T, 'dp', axis=0, tiled=True, axis_i...  23.8 us
    dot_general x7, matrix products, first_product(): jnp.dot(part_of(place), first[place], preferred_element_type=jnp.float32)  18.7 us
    ppermute x1, starting transfers between devices, swap_cores(): return lax.ppermute(value, 'fsdp', inner_pairs(Y_SIDE * CORES, CORES, 1))  17 us
    ppermute x8, starting transfers between devices, send_z(): return lax.ppermute(value, 'dp', ring_pairs(Z_SIDE * X_SIDE, X_SIDE, step))  13.3 us
    ppermute x4, waiting for transfers between devices, send_y(): return lax.ppermute(value, 'fsdp', ring_pairs(Y_SIDE * CORES, CORES, step))  12.4 us
    pallas_call x1, Pallas kernels, second_products(): pl.pallas_call(second_kernel, out_shape=(shape, shape), in_specs=[whole]...  12.4 us
  transfers between devices with their start and end apart: 27, of which 16 were waited for; matrix products, arithmetic and copies ran while one was open for 18% of the time, Pallas kernels for 4%

profile of v1, /device:TPU:1, one launch (start us, length us, event | category | flops | bytes accessed | tf_op | source)
XLA Modules:
  0.0 276.1 jit_solution(1480058197936727692)
XLA Ops:
  7.2 3.4 %collective-permute-start = (bf16[96,1536]{1,0:T(8,128)(2,1)}, bf16[96,1536]{1,0:T(8,128)(2,1)S(1)}, u32[]{:S(2)}, u32[]{:S(2)}) collective-permute-start(bf16[96,1536]{1,0:T(8,128)(2,1)} %param.24), channel_id=1, source_target_pairs={{0,24},{8,0},{16,8},{24,16},{32,56},{40,32},{48,40},{56,48},{64,88... | collective-permute-start | bytes 884744 | tf_op jit(solution)/shard_map/ppermute | solution.py:92
  11.8 1.2 convert_reduce_fusion.50
  13.0 1.1 convert_reduce_fusion.49
  15.1 1.1 convert_element_type.591
  16.2 5.0 %convert_reduce_fusion = (f32[8,8,8]{2,1,0:T(8,128)S(1)}, f32[8,8,8]{2,1,0:T(8,128)S(1)}, bf16[8,8,8,384]{3,2,1,0:T(8,128)(2,1)S(1)}) fusion(f32[384]{0:T(512)S(1)} %copy-done.18, f32[384]{0:T(512)S(1)} %get-tuple-element.129, f32[384]{0:T(512)S(1)} %get-tuple-element.130, f32[384]{0:T(512)S(1)} %get-tuple-element.83, f32[384]{0:T(512)S(1)} %get-tuple-element.84, ...), kind=kLoop, calls=%fused_computation.63 | loop fusion | flops 20249600 | bytes 1260544 | tf_op jit(solution)/shard_map/reduce_sum | solution.py:248
  23.8 1.1 broadcast_in_dim.27
  26.4 1.2 collective-permute-done.2
  28.2 5.0 %all-to-all-start = ((f32[8,2,512]{2,1,0:T(2,128)}), f32[8,2,512]{2,1,0:T(2,128)S(1)}, u32[]{:S(2)}, u32[]{:S(2)}) async-start(f32[8,2,512]{2,1,0:T(2,128)} %broadcast_in_dim.32), calls=%async_computation | async-start | bytes 65536 | tf_op jit(solution)/shard_map/all_to_all | solution.py:57
  35.4 5.6 %collective-permute-start.3 = (bf16[384,1536]{1,0:T(8,128)(2,1)}, bf16[384,1536]{1,0:T(8,128)(2,1)}, u32[]{:S(2)}, u32[]{:S(2)}) collective-permute-start(bf16[384,1536]{1,0:T(8,128)(2,1)} %bitcast.5), channel_id=1, source_target_pairs={{0,224},{8,232},{16,240},{24,248},{32,0},{40,8},{48,16},{56,24},{6... | collective-permute-start | bytes 3538952 | tf_op jit(solution)/shard_map/ppermute | solution.py:88
  42.0 23.8 %all-gather.5.cloned.1.call-done = bf16[768,1536]{1,0:T(8,128)(2,1)} async-done(((bf16[96,1536]{1,0:T(8,128)(2,1)}), bf16[768,1536]{1,0:T(8,128)(2,1)}) %all-gather.5.cloned.1.call-update) | async-done | bytes 2359312 | tf_op jit(solution)/shard_map/all_gather | solution.py:242
  65.8 1.8 fusion.201
  67.6 10.4 %collective-permute-done.3 = bf16[384,1536]{1,0:T(8,128)(2,1)} collective-permute-done((bf16[384,1536]{1,0:T(8,128)(2,1)}, bf16[384,1536]{1,0:T(8,128)(2,1)}, u32[]{:S(2)}, u32[]{:S(2)}) %collective-permute-start.3) | collective-permute-done | bytes 1179680 | tf_op jit(solution)/shard_map/ppermute | solution.py:88
  78.9 1.9 collective-permute-start.5
  80.8 1.2 collective-permute-start.7
  81.9 1.5 collective-permute-start.8
  83.4 22.7 %collective-permute-done.5 = bf16[384,1536]{1,0:T(8,128)(2,1)S(1)} collective-permute-done((bf16[384,1536]{1,0:T(8,128)(2,1)}, bf16[384,1536]{1,0:T(8,128)(2,1)S(1)}, u32[]{:S(2)}, u32[]{:S(2)}) %collective-permute-start.5) | collective-permute-done | bytes 1179680 | tf_op jit(solution)/shard_map/ppermute | solution.py:88
  106.1 2.6 collective-permute-done.6
  112.9 1.8 collective-permute-start.12
  114.7 2.7 collective-permute-start.9
  117.4 2.5 fusion.132
  121.0 2.3 fusion.136
  123.3 2.3 fusion.134
  125.6 4.1 %fusion.3 = f32[512,1536]{1,0:T(8,128)} fusion(f32[512,1536]{1,0:T(8,128)S(1)} %fusion.130, f32[512,1536]{1,0:T(8,128)S(1)} %fusion.132, f32[512,1536]{1,0:T(8,128)S(1)} %fusion.134, f32[512,1536]{1,0:T(8,128)S(1)} %fusion.136, bf16[384,1536]{1,0:T(8,128)(2,1)} %bitcast.5, f32[1536]{0:T(1024)S(1)} %copy-done.16, bf16[8,512,384]{2,1,0:T(8,128)(2,1)S(1)} %bitcast.132, ...), kind=kOutput, calls=%fused_computation.52 | convolution fusion | flops 607911936 | bytes 17309700 | tf_op jit(solution)/shard_map/dot_general | solution.py:302
  129.6 11.9 %collective-permute-done.11.rest_7_ = bf16[384,1536]{1,0:T(8,128)(2,1)} collective-permute-done((bf16[384,1536]{1,0:T(8,128)(2,1)S(1)}, bf16[384,1536]{1,0:T(8,128)(2,1)}, u32[]{:S(2)}, u32[]{:S(2)}) %collective-permute-start.11) | collective-permute-done | bytes 1179680 | tf_op jit(solution)/shard_map/ppermute | solution.py:92
  141.6 4.3 %collective-permute-done.10 = bf16[384,1536]{1,0:T(8,128)(2,1)} collective-permute-done((bf16[384,1536]{1,0:T(8,128)(2,1)}, bf16[384,1536]{1,0:T(8,128)(2,1)}, u32[]{:S(2)}, u32[]{:S(2)}) %collective-permute-start.10) | collective-permute-done | bytes 1179680 | tf_op jit(solution)/shard_map/ppermute | solution.py:88
  146.8 1.1 slice.504
  148.0 1.1 slice.505
  149.1 3.0 %collective-permute-start.14 = (bf16[192,1536]{1,0:T(8,128)(2,1)S(1)}, bf16[192,1536]{1,0:T(8,128)(2,1)S(1)}, u32[]{:S(2)}, u32[]{:S(2)}) collective-permute-start(bf16[192,1536]{1,0:T(8,128)(2,1)S(1)} %slice.505), channel_id=1, source_target_pairs={{0,224},{8,232},{16,240},{24,248},{32,0},{40,8},{48,16},{56,24},{6... | collective-permute-start | bytes 1769480 | tf_op jit(solution)/shard_map/ppermute | solution.py:88
  152.2 2.5 fusion.128
  154.7 1.0 dynamic-slice_bitcast_fusion.part_ref
  155.8 4.2 %add_add_fusion.preact_ref = f32[512,1536]{1,0:T(8,128)} fusion(f32[512,1536]{1,0:T(8,128)S(1)} %copy-done.5, f32[512,1536]{1,0:T(8,128)S(1)} %fusion.128, bf16[384,1536]{1,0:T(8,128)(2,1)} %collective-permute-done.10, bf16[8,512,384]{2,1,0:T(8,128)(2,1)} %bitcast.128, s32[]{:T(128)S(6)} %select_n.201), kind=kOutput, calls=%fused_computation.57 | convolution fusion | flops 605552640 | bytes 11010052 | tf_op jit(solution)/shard_map/dot_general | solution.py:302
  159.9 7.4 %collective-permute-done.15.rest_4_ = bf16[384,1536]{1,0:T(8,128)(2,1)} collective-permute-done((bf16[384,1536]{1,0:T(8,128)(2,1)}, bf16[384,1536]{1,0:T(8,128)(2,1)}, u32[]{:S(2)}, u32[]{:S(2)}) %collective-permute-start.15) | collective-permute-done | bytes 1179680 | tf_op jit(solution)/shard_map/ppermute | solution.py:92
  167.3 3.6 %collective-permute-done.16.rest_5_ = bf16[384,1536]{1,0:T(8,128)(2,1)} collective-permute-done((bf16[384,1536]{1,0:T(8,128)(2,1)}, bf16[384,1536]{1,0:T(8,128)(2,1)}, u32[]{:S(2)}, u32[]{:S(2)}) %collective-permute-start.16) | collective-permute-done | bytes 1179680 | tf_op jit(solution)/shard_map/ppermute | solution.py:92
  170.9 12.4 %shard_map.202 = (bf16[4,4,96,512]{3,2,1,0:T(8,128)(2,1)}, bf16[4,4,96,512]{3,2,1,0:T(8,128)(2,1)}) custom-call(f32[512,1536]{1,0:T(8,128)} %add_add_fusion.preact_ref, bf16[512,384]{1,0:T(8,128)(2,1)S(1)} %dynamic-slice_bitcast_fusion.part_ref, bf16[192,1536]{1,0:T(8,128)(2,1)S(1)} %collective-permute-done.13.low_ref, ...), custom_call_target="tpu_custom_call" | custom-call | flops 4831838208 | bytes 11796480 | tf_op jit(solution)/shard_map/pallas_call | solution.py:164
  183.3 17.0 %collective-permute-start.17 = (bf16[4,384,512]{2,1,0:T(8,128)(2,1)}, bf16[4,384,512]{2,1,0:T(8,128)(2,1)S(1)}, u32[]{:S(2)}, u32[]{:S(2)}) collective-permute-start(bf16[4,384,512]{2,1,0:T(8,128)(2,1)} %bitcast.152), channel_id=1, source_target_pairs={{0,1},{1,0},{2,3},{3,2},{4,5},{5,4},{6,7},{7,6},{8,9},{9,8},{10,11... | collective-permute-start | bytes 4718600 | tf_op jit(solution)/shard_map/ppermute | solution.py:100
  200.3 3.2 %collective-permute-done.17 = bf16[4,384,512]{2,1,0:T(8,128)(2,1)S(1)} collective-permute-done((bf16[4,384,512]{2,1,0:T(8,128)(2,1)}, bf16[4,384,512]{2,1,0:T(8,128)(2,1)S(1)}, u32[]{:S(2)}, u32[]{:S(2)}) %collective-permute-start.17) | collective-permute-done | bytes 1572896 | tf_op jit(solution)/shard_map/ppermute | solution.py:100
  203.6 1.5 convert_add_fusion.1
  205.1 3.4 %collective-permute-start.18 = (bf16[192,512]{1,0:T(8,128)(2,1)S(1)}, bf16[192,512]{1,0:T(8,128)(2,1)S(1)}, u32[]{:S(2)}, u32[]{:S(2)}) collective-permute-start(bf16[192,512]{1,0:T(8,128)(2,1)S(1)} %get-tuple-element.149), channel_id=1, source_target_pairs={{0,2},{1,3},{2,4},{3,5},{4,6},{5,7},{6,0},{7,1},{8,10},{9,11},{10,... | collective-permute-start | bytes 589832 | tf_op jit(solution)/shard_map/ppermute | solution.py:96
  209.2 4.8 %collective-permute-done.18 = bf16[192,512]{1,0:T(8,128)(2,1)S(1)} collective-permute-done((bf16[192,512]{1,0:T(8,128)(2,1)S(1)}, bf16[192,512]{1,0:T(8,128)(2,1)S(1)}, u32[]{:S(2)}, u32[]{:S(2)}) %collective-permute-start.18) | collective-permute-done | bytes 196640 | tf_op jit(solution)/shard_map/ppermute | solution.py:96
  215.6 2.1 collective-permute-start.21
  217.7 7.4 %collective-permute-done.19 = bf16[384,512]{1,0:T(8,128)(2,1)S(1)} collective-permute-done((bf16[384,512]{1,0:T(8,128)(2,1)S(1)}, bf16[384,512]{1,0:T(8,128)(2,1)S(1)}, u32[]{:S(2)}, u32[]{:S(2)}) %collective-permute-start.19) | collective-permute-done | bytes 393248 | tf_op jit(solution)/shard_map/ppermute | solution.py:96
  225.2 1.2 fusion.118
  229.9 6.9 %all-to-all-start.1 = ((f32[8,11,768]{2,1,0:T(8,128)}), f32[8,11,768]{2,1,0:T(8,128)S(1)}, u32[]{:S(2)}, u32[]{:S(2)}) async-start(f32[8,11,768]{2,1,0:T(8,128)} %broadcast_in_dim.34), calls=%async_computation.1 | async-start | bytes 786432 | tf_op jit(solution)/shard_map/all_to_all | solution.py:57
  238.1 6.7 %all-to-all-done.1 = f32[8,11,768]{2,1,0:T(8,128)S(1)} async-done(((f32[8,11,768]{2,1,0:T(8,128)}), f32[8,11,768]{2,1,0:T(8,128)S(1)}, u32[]{:S(2)}, u32[]{:S(2)}) %all-to-all-start.1) | async-done | bytes 270368 | tf_op jit(solution)/shard_map/all_to_all | solution.py:57
  245.7 3.6 %fusion.205 = (f32[8]{0:T(128)S(1)}, f32[8,2048]{1,0:T(8,128)S(1)}) fusion(f32[]{:T(128)} %bitcast.40, bf16[8,768]{1,0:T(8,128)(2,1)S(1)} %fusion.155, bf16[2048,1536]{1,0:T(8,128)(2,1)} %all-gather.7.cloned.1.call-done), kind=kOutput, calls=%fused_computation.381 | convolution fusion | flops 25198584 | bytes 3224096 | tf_op jit(solution)/shard_map/dot_general | solution.py:48
  249.3 3.6 %fusion.204 = (f32[8]{0:T(128)S(1)}, f32[8,2048]{1,0:T(8,128)S(1)}) fusion(f32[]{:T(128)} %bitcast.40, bf16[2048,1536]{1,0:T(8,128)(2,1)} %all-gather.7.cloned.1.call-done, f32[8,768]{1,0:T(8,128)S(1)} %get-tuple-element.138, f32[8]{0:T(128)S(1)} %add_sqrt_fusion.1), kind=kOutput, calls=%fused_computation.380 | convolution fusion | flops 25210872 | bytes 3236416 | tf_op jit(solution)/shard_map/dot_general | solution.py:48
  253.2 7.8 %all_to_all.15 = f32[8,1,6]{2,1,0:T(1,128)S(1)} all-to-all(f32[8,1,6]{2,1,0:T(1,128)S(1)} %copy.76), channel_id=1, replica_groups=mesh['dp'=32,'fsdp'=8] {'fsdp'}, dimensions={0} | all-to-all | bytes 384 | tf_op jit(solution)/shard_map/all_to_all | solution.py:365
  261.8 2.1 slice_reduce_fusion.1
  (150 shorter events, 25.5 us)
Async XLA Ops:
  7.2 16.3 %copy-start = (bf16[384,768]{1,0:T(8,128)(2,1)S(1)}, bf16[384,768]{1,0:T(8,128)(2,1)}, u32[]{:S(2)}) copy-start(bf16[384,768]{1,0:T(8,128)(2,1)} %param.31) | copy-start | bytes 1769476
  7.2 9.0 %copy-start.18 = (f32[384]{0:T(512)S(1)}, f32[384]{0:T(512)}, u32[]{:S(2)}) copy-start(f32[384]{0:T(512)} %param.21) | copy-start | bytes 4612
  7.2 58.6 %all-gather.5.cloned.1.call-start = ((), (), s32[]{:S(2)}) async-start(), calls=%async_computation.3 | async-start | bytes 2654208 | tf_op jit(solution)/shard_map/all_gather | solution.py:242
  7.2 19.2 %collective-permute-start = (bf16[96,1536]{1,0:T(8,128)(2,1)}, bf16[96,1536]{1,0:T(8,128)(2,1)S(1)}, u32[]{:S(2)}, u32[]{:S(2)}) collective-permute-start(bf16[96,1536]{1,0:T(8,128)(2,1)} %param.24), channel_id=1, source_target_pairs={{0,24},{8,0},{16,8},{24,16},{32,56},{40,32},{48,40},{56,48},{64,88... | collective-permute-start | bytes 884744 | tf_op jit(solution)/shard_map/ppermute | solution.py:92
  10.6 15.8 %collective-permute-start.1 = (bf16[96,1536]{1,0:T(8,128)(2,1)}, bf16[96,1536]{1,0:T(8,128)(2,1)S(1)}, u32[]{:S(2)}, u32[]{:S(2)}) collective-permute-start(bf16[96,1536]{1,0:T(8,128)(2,1)} %param.24), channel_id=1, source_target_pairs={{0,16},{8,24},{16,0},{24,8},{32,48},{40,56},{48,32},{56,40},{64,80... | collective-permute-start | bytes 884744 | tf_op jit(solution)/shard_map/ppermute | solution.py:92
  11.1 16.4 %collective-permute-start.2 = (bf16[96,1536]{1,0:T(8,128)(2,1)}, bf16[96,1536]{1,0:T(8,128)(2,1)S(1)}, u32[]{:S(2)}, u32[]{:S(2)}) collective-permute-start(bf16[96,1536]{1,0:T(8,128)(2,1)} %param.24), channel_id=1, source_target_pairs={{0,8},{8,16},{16,24},{24,0},{32,40},{40,48},{48,56},{56,32},{64,72... | collective-permute-start | bytes 884744 | tf_op jit(solution)/shard_map/ppermute | solution.py:92
  11.8 11.2 %copy-start.17 = (f32[384]{0:T(512)S(1)}, f32[384]{0:T(512)}, u32[]{:S(2)}) copy-start(f32[384]{0:T(512)} %param.29) | copy-start | bytes 4612
  11.8 11.2 %copy-start.21 = (f32[384]{0:T(512)S(1)}, f32[384]{0:T(512)}, u32[]{:S(2)}) copy-start(f32[384]{0:T(512)} %param.30) | copy-start | bytes 4612
  11.8 11.2 %copy-start.12 = (bf16[64,768]{1,0:T(8,128)(2,1)S(1)}, bf16[64,768]{1,0:T(8,128)(2,1)}, u32[]{:S(2)}) copy-start(bf16[64,768]{1,0:T(8,128)(2,1)} %param.33) | copy-start | bytes 294916
  11.8 11.3 %copy-start.11 = (bf16[64,768]{1,0:T(8,128)(2,1)S(1)}, bf16[64,768]{1,0:T(8,128)(2,1)}, u32[]{:S(2)}) copy-start(bf16[64,768]{1,0:T(8,128)(2,1)} %param.32) | copy-start | bytes 294916
  13.0 10.3 %copy-start.14 = (bf16[8,768]{1,0:T(8,128)(2,1)S(1)}, bf16[8,768]{1,0:T(8,128)(2,1)}, u32[]{:S(2)}) copy-start(bf16[8,768]{1,0:T(8,128)(2,1)} %param.34) | copy-start | bytes 36868
  21.2 3.8 %copy-start.13 = (bf16[96,1536]{1,0:T(8,128)(2,1)S(1)}, bf16[96,1536]{1,0:T(8,128)(2,1)}, u32[]{:S(2)}) copy-start(bf16[96,1536]{1,0:T(8,128)(2,1)} %param.24) | copy-start | bytes 884740
  28.2 12.8 %all-to-all-start = ((f32[8,2,512]{2,1,0:T(2,128)}), f32[8,2,512]{2,1,0:T(2,128)S(1)}, u32[]{:S(2)}, u32[]{:S(2)}) async-start(f32[8,2,512]{2,1,0:T(2,128)} %broadcast_in_dim.32), calls=%async_computation | async-start | bytes 65536 | tf_op jit(solution)/shard_map/all_to_all | solution.py:57
  33.2 84.2 %all-gather.9.cloned.1.call-start = ((), (), s32[]{:S(2)}) async-start(), calls=%async_computation.5 | async-start | bytes 3538944 | tf_op jit(solution)/shard_map/all_gather | solution.py:290
  35.4 42.6 %collective-permute-start.3 = (bf16[384,1536]{1,0:T(8,128)(2,1)}, bf16[384,1536]{1,0:T(8,128)(2,1)}, u32[]{:S(2)}, u32[]{:S(2)}) collective-permute-start(bf16[384,1536]{1,0:T(8,128)(2,1)} %bitcast.5), channel_id=1, source_target_pairs={{0,224},{8,232},{16,240},{24,248},{32,0},{40,8},{48,16},{56,24},{6... | collective-permute-start | bytes 3538952 | tf_op jit(solution)/shard_map/ppermute | solution.py:88
  41.0 37.8 %collective-permute-start.4 = (bf16[384,1536]{1,0:T(8,128)(2,1)}, bf16[384,1536]{1,0:T(8,128)(2,1)}, u32[]{:S(2)}, u32[]{:S(2)}) collective-permute-start(bf16[384,1536]{1,0:T(8,128)(2,1)} %bitcast.5), channel_id=1, source_target_pairs={{0,32},{8,40},{16,48},{24,56},{32,64},{40,72},{48,80},{56,88},{64,... | collective-permute-start | bytes 3538952 | tf_op jit(solution)/shard_map/ppermute | solution.py:88
  78.8 166.9 %all-gather.7.cloned.1.call-start = ((), (), s32[]{:S(2)}) async-start(), calls=%async_computation.4 | async-start | bytes 6488064 | tf_op jit(solution)/shard_map/all_gather | solution.py:296
  78.9 27.2 %collective-permute-start.5 = (bf16[384,1536]{1,0:T(8,128)(2,1)}, bf16[384,1536]{1,0:T(8,128)(2,1)S(1)}, u32[]{:S(2)}, u32[]{:S(2)}) collective-permute-start(bf16[384,1536]{1,0:T(8,128)(2,1)} %collective-permute-done.3), channel_id=1, source_target_pairs={{0,224},{8,232},{16,240},{24,248},{32,0},{40,8},{48,16},{56,24},{6... | collective-permute-start | bytes 3538952 | tf_op jit(solution)/shard_map/ppermute | solution.py:88
  80.7 27.9 %collective-permute-start.6 = (bf16[384,1536]{1,0:T(8,128)(2,1)}, bf16[384,1536]{1,0:T(8,128)(2,1)S(1)}, u32[]{:S(2)}, u32[]{:S(2)}) collective-permute-start(bf16[384,1536]{1,0:T(8,128)(2,1)} %collective-permute-done.4), channel_id=1, source_target_pairs={{0,32},{8,40},{16,48},{24,56},{32,64},{40,72},{48,80},{56,88},{64,... | collective-permute-start | bytes 3538952 | tf_op jit(solution)/shard_map/ppermute | solution.py:88
  80.8 27.9 %collective-permute-start.7 = (bf16[384,1536]{1,0:T(8,128)(2,1)S(1)}, bf16[384,1536]{1,0:T(8,128)(2,1)S(1)}, u32[]{:S(2)}, u32[]{:S(2)}) collective-permute-start(bf16[384,1536]{1,0:T(8,128)(2,1)S(1)} %get-tuple-element.46.rest_0_), channel_id=1, source_target_pairs={{0,8},{8,16},{16,24},{24,0},{32,40},{40,48},{48,56},{56,32},{64,72... | collective-permute-start | bytes 3538952 | tf_op jit(solution)/shard_map/ppermute | solution.py:92
  81.9 28.8 %collective-permute-start.8 = (bf16[384,1536]{1,0:T(8,128)(2,1)S(1)}, bf16[384,1536]{1,0:T(8,128)(2,1)S(1)}, u32[]{:S(2)}, u32[]{:S(2)}) collective-permute-start(bf16[384,1536]{1,0:T(8,128)(2,1)S(1)} %get-tuple-element.46.rest_0_), channel_id=1, source_target_pairs={{0,24},{8,0},{16,8},{24,16},{32,56},{40,32},{48,40},{56,48},{64,88... | collective-permute-start | bytes 3538952 | tf_op jit(solution)/shard_map/ppermute | solution.py:92
  106.1 2.6 copy-start.8
  108.7 1.0 copy-start.9
  109.7 1.0 copy-start.1
  110.7 1.0 copy-start.3
  111.9 29.6 %collective-permute-start.11 = (bf16[384,1536]{1,0:T(8,128)(2,1)S(1)}, bf16[384,1536]{1,0:T(8,128)(2,1)}, u32[]{:S(2)}, u32[]{:S(2)}) collective-permute-start(bf16[384,1536]{1,0:T(8,128)(2,1)S(1)} %get-tuple-element.53.rest_1_), channel_id=1, source_target_pairs={{0,8},{8,16},{16,24},{24,0},{32,40},{40,48},{48,56},{56,32},{64,72... | collective-permute-start | bytes 3538952 | tf_op jit(solution)/shard_map/ppermute | solution.py:92
  112.9 28.7 %collective-permute-start.12 = (bf16[384,1536]{1,0:T(8,128)(2,1)S(1)}, bf16[384,1536]{1,0:T(8,128)(2,1)}, u32[]{:S(2)}, u32[]{:S(2)}) collective-permute-start(bf16[384,1536]{1,0:T(8,128)(2,1)S(1)} %get-tuple-element.53.rest_1_), channel_id=1, source_target_pairs={{0,24},{8,0},{16,8},{24,16},{32,56},{40,32},{48,40},{56,48},{64,88... | collective-permute-start | bytes 3538952 | tf_op jit(solution)/shard_map/ppermute | solution.py:92
  114.7 31.3 %collective-permute-start.10 = (bf16[384,1536]{1,0:T(8,128)(2,1)}, bf16[384,1536]{1,0:T(8,128)(2,1)}, u32[]{:S(2)}, u32[]{:S(2)}) collective-permute-start(bf16[384,1536]{1,0:T(8,128)(2,1)} %copy-done.9), channel_id=1, source_target_pairs={{0,32},{8,40},{16,48},{24,56},{32,64},{40,72},{48,80},{56,88},{64,... | collective-permute-start | bytes 3538952 | tf_op jit(solution)/shard_map/ppermute | solution.py:88
  114.7 31.3 %collective-permute-start.9 = (bf16[384,1536]{1,0:T(8,128)(2,1)}, bf16[384,1536]{1,0:T(8,128)(2,1)}, u32[]{:S(2)}, u32[]{:S(2)}) collective-permute-start(bf16[384,1536]{1,0:T(8,128)(2,1)} %copy-done.8), channel_id=1, source_target_pairs={{0,224},{8,232},{16,240},{24,248},{32,0},{40,8},{48,16},{56,24},{6... | collective-permute-start | bytes 3538952 | tf_op jit(solution)/shard_map/ppermute | solution.py:88
  117.3 50.0 %collective-permute-start.15 = (bf16[384,1536]{1,0:T(8,128)(2,1)}, bf16[384,1536]{1,0:T(8,128)(2,1)}, u32[]{:S(2)}, u32[]{:S(2)}) collective-permute-start(bf16[384,1536]{1,0:T(8,128)(2,1)} %copy-done.1), channel_id=1, source_target_pairs={{0,8},{8,16},{16,24},{24,0},{32,40},{40,48},{48,56},{56,32},{64,72... | collective-permute-start | bytes 3538952 | tf_op jit(solution)/shard_map/ppermute | solution.py:92
  117.3 2.5 copy-start.6
  117.4 2.7 copy-start.10
  123.3 2.3 copy-start.16
  145.9 25.0 %collective-permute-start.16 = (bf16[384,1536]{1,0:T(8,128)(2,1)}, bf16[384,1536]{1,0:T(8,128)(2,1)}, u32[]{:S(2)}, u32[]{:S(2)}) collective-permute-start(bf16[384,1536]{1,0:T(8,128)(2,1)} %collective-permute-done.12.rest_3_), channel_id=1, source_target_pairs={{0,24},{8,0},{16,8},{24,16},{32,56},{40,32},{48,40},{56,48},{64,88... | collective-permute-start | bytes 3538952 | tf_op jit(solution)/shard_map/ppermute | solution.py:92
  147.9 19.4 %collective-permute-start.13 = (bf16[192,1536]{1,0:T(8,128)(2,1)S(1)}, bf16[192,1536]{1,0:T(8,128)(2,1)S(1)}, u32[]{:S(2)}, u32[]{:S(2)}) collective-permute-start(bf16[192,1536]{1,0:T(8,128)(2,1)S(1)} %slice.504), channel_id=1, source_target_pairs={{0,32},{8,40},{16,48},{24,56},{32,64},{40,72},{48,80},{56,88},{64,... | collective-permute-start | bytes 1769480 | tf_op jit(solution)/shard_map/ppermute | solution.py:88
  149.1 18.2 %collective-permute-start.14 = (bf16[192,1536]{1,0:T(8,128)(2,1)S(1)}, bf16[192,1536]{1,0:T(8,128)(2,1)S(1)}, u32[]{:S(2)}, u32[]{:S(2)}) collective-permute-start(bf16[192,1536]{1,0:T(8,128)(2,1)S(1)} %slice.505), channel_id=1, source_target_pairs={{0,224},{8,232},{16,240},{24,248},{32,0},{40,8},{48,16},{56,24},{6... | collective-permute-start | bytes 1769480 | tf_op jit(solution)/shard_map/ppermute | solution.py:88
  152.2 3.6 %copy-start.5 = (f32[512,1536]{1,0:T(8,128)S(1)}, f32[512,1536]{1,0:T(8,128)}, u32[]{:S(2)}) copy-start(f32[512,1536]{1,0:T(8,128)} %fusion.3) | copy-start | bytes 9437188
  155.7 15.2 %copy-start.2 = (bf16[384,1536]{1,0:T(8,128)(2,1)S(1)}, bf16[384,1536]{1,0:T(8,128)(2,1)}, u32[]{:S(2)}) copy-start(bf16[384,1536]{1,0:T(8,128)(2,1)} %copy-done.1) | copy-start | bytes 3538948
  155.7 15.2 %copy-start.4 = (bf16[384,1536]{1,0:T(8,128)(2,1)S(1)}, bf16[384,1536]{1,0:T(8,128)(2,1)}, u32[]{:S(2)}) copy-start(bf16[384,1536]{1,0:T(8,128)(2,1)} %copy-done.3) | copy-start | bytes 3538948
  183.3 20.2 %collective-permute-start.17 = (bf16[4,384,512]{2,1,0:T(8,128)(2,1)}, bf16[4,384,512]{2,1,0:T(8,128)(2,1)S(1)}, u32[]{:S(2)}, u32[]{:S(2)}) collective-permute-start(bf16[4,384,512]{2,1,0:T(8,128)(2,1)} %bitcast.152), channel_id=1, source_target_pairs={{0,1},{1,0},{2,3},{3,2},{4,5},{5,4},{6,7},{7,6},{8,9},{9,8},{10,11... | collective-permute-start | bytes 4718600 | tf_op jit(solution)/shard_map/ppermute | solution.py:100
  205.1 8.9 %collective-permute-start.18 = (bf16[192,512]{1,0:T(8,128)(2,1)S(1)}, bf16[192,512]{1,0:T(8,128)(2,1)S(1)}, u32[]{:S(2)}, u32[]{:S(2)}) collective-permute-start(bf16[192,512]{1,0:T(8,128)(2,1)S(1)} %get-tuple-element.149), channel_id=1, source_target_pairs={{0,2},{1,3},{2,4},{3,5},{4,6},{5,7},{6,0},{7,1},{8,10},{9,11},{10,... | collective-permute-start | bytes 589832 | tf_op jit(solution)/shard_map/ppermute | solution.py:96
  208.5 6.3 %collective-permute-start.20 = (bf16[192,512]{1,0:T(8,128)(2,1)S(1)}, bf16[192,512]{1,0:T(8,128)(2,1)S(1)}, u32[]{:S(2)}, u32[]{:S(2)}) collective-permute-start(bf16[192,512]{1,0:T(8,128)(2,1)S(1)} %get-tuple-element.150), channel_id=1, source_target_pairs={{0,6},{1,7},{2,0},{3,1},{4,2},{5,3},{6,4},{7,5},{8,14},{9,15},{10,... | collective-permute-start | bytes 589832 | tf_op jit(solution)/shard_map/ppermute | solution.py:96
  214.1 11.0 %collective-permute-start.19 = (bf16[384,512]{1,0:T(8,128)(2,1)S(1)}, bf16[384,512]{1,0:T(8,128)(2,1)S(1)}, u32[]{:S(2)}, u32[]{:S(2)}) collective-permute-start(bf16[384,512]{1,0:T(8,128)(2,1)S(1)} %pad_maximum_fusion), channel_id=1, source_target_pairs={{0,2},{1,3},{2,4},{3,5},{4,6},{5,7},{6,0},{7,1},{8,10},{9,11},{10,... | collective-permute-start | bytes 1179656 | tf_op jit(solution)/shard_map/ppermute | solution.py:96
  215.6 9.6 %collective-permute-start.21 = (bf16[384,512]{1,0:T(8,128)(2,1)}, bf16[384,512]{1,0:T(8,128)(2,1)S(1)}, u32[]{:S(2)}, u32[]{:S(2)}) collective-permute-start(bf16[384,512]{1,0:T(8,128)(2,1)} %pad_maximum_fusion.1), channel_id=1, source_target_pairs={{0,6},{1,7},{2,0},{3,1},{4,2},{5,3},{6,4},{7,5},{8,14},{9,15},{10,... | collective-permute-start | bytes 1179656 | tf_op jit(solution)/shard_map/ppermute | solution.py:96
  227.4 10.0 %copy-start.23 = (f32[64]{0:T(128)S(1)}, f32[64]{0:T(128)}, u32[]{:S(2)}) copy-start(f32[64]{0:T(128)} %param.35) | copy-start | bytes 772
  227.4 10.6 %copy-start.22 = (s32[256]{0:T(256)S(1)}, s32[256]{0:T(256)}, u32[]{:S(2)}) copy-start(s32[256]{0:T(256)} %param.37) | copy-start | bytes 3076
  229.9 15.0 %all-to-all-start.1 = ((f32[8,11,768]{2,1,0:T(8,128)}), f32[8,11,768]{2,1,0:T(8,128)S(1)}, u32[]{:S(2)}, u32[]{:S(2)}) async-start(f32[8,11,768]{2,1,0:T(8,128)} %broadcast_in_dim.34), calls=%async_computation.1 | async-start | bytes 786432 | tf_op jit(solution)/shard_map/all_to_all | solution.py:57
  245.7 3.6 %copy-start.15 = (f32[8,768]{1,0:T(8,128)}, f32[8,768]{1,0:T(8,128)S(1)}, u32[]{:S(2)}) copy-start(f32[8,768]{1,0:T(8,128)S(1)} %get-tuple-element.138) | copy-start | bytes 73732
  (3 other events, 3.0 us)
Sparse Core Ops, SparseCore 0:
  11.9 53.8 all-gather.4
  79.0 29.1 all-gather.8
  111.9 96.4 all-gather.6
